TPU v7x, 1024 devices: a whole 8x8x8 slice. The times are simulated.
1024 devices in a mesh: node: 64 (over z, y), local: 16 (over x, core).
Axes of the slice: x: 8, y: 8, z: 8, core: 2. Of those that a mesh axis runs over, the one named last changes fastest.
Arguments:
- tokens: bfloat16 [8192, 7168], P('node', 'local'), may hold values from -6 to 6
- route_expert: int32 [8192], P('node'), may hold values from 0 to 15, as said below
- hidden_grad: bfloat16 [8192, 2048], P('node'), may hold values from -6 to 6
- gate_weight: bfloat16 [7168, 32768], P('local', 'node'), may hold values from -0.0625 to 0.0625
- up_weight: bfloat16 [7168, 32768], P('local', 'node'), may hold values from -0.0625 to 0.0625
Outputs:
- token_grad: bfloat16 [8192, 7168], P('node', 'local')
- gate_grad: float32 [7168, 32768], P('local', 'node')
- up_grad: float32 [7168, 32768], P('local', 'node')
Inputs may be any that keep to these rules, and one draw needn't show every extreme that they name: `route_expert`: at most 10 of the 128 tokens of one index of node name the same expert; on every index of node exactly 10 of its tokens name one expert, the same expert on all of them.
All inputs are finite; a program needn't handle non-finite values.
Results may differ from a plain program's by a relative error of at most 0.0058.
Values may be sent and summed in bfloat16 or wider, within the bound.
A program may use at most 32 MiB of HBM per device.

v0:
```python
import jax
import jax.numpy as jnp
from jax import lax
from jax.sharding import PartitionSpec as P


def activate(gate_pre, up_pre, hidden_rows):
    sigmoid_gate = jax.nn.sigmoid(gate_pre)
    activated = gate_pre * sigmoid_gate
    slope_gate = sigmoid_gate * (1.0 + gate_pre * (1.0 - sigmoid_gate))
    grad_up = (hidden_rows * activated).astype(jnp.bfloat16)
    grad_gate = (hidden_rows * up_pre * slope_gate).astype(jnp.bfloat16)
    return (grad_gate, grad_up)


def shards(tokens, route_expert, hidden_grad, gate_weight, up_weight):
    node_count = lax.axis_size("node")
    local_count = lax.axis_size("local")
    tok_count = tokens.shape[0]
    feature_width = tokens.shape[1]
    part_width = gate_weight.shape[1]
    group_size = hidden_grad.shape[1] // part_width
    experts = node_count // group_size
    capacity = min(tok_count, max(2, (5 * tok_count + 4 * experts - 1) // (4 * experts)))
    onehot = (route_expert[:, None] == jnp.arange(experts, dtype=jnp.int32)[None, :]).astype(
        jnp.int32
    )
    rank_of = jnp.sum((jnp.cumsum(onehot, axis=0) - onehot) * onehot, axis=1)
    slot_of = route_expert * capacity + rank_of
    select = (slot_of[None, :] == jnp.arange(experts * capacity, dtype=jnp.int32)[:, None]).astype(
        jnp.bfloat16
    )
    send_rows = jnp.dot(select, tokens, preferred_element_type=jnp.float32).astype(jnp.bfloat16)
    send_grads = jnp.dot(select, hidden_grad, preferred_element_type=jnp.float32).astype(
        jnp.bfloat16
    )
    rows_nodes = jnp.broadcast_to(
        send_rows.reshape(experts, 1, capacity, feature_width),
        (experts, group_size, capacity, feature_width),
    ).reshape(node_count, capacity, feature_width)
    grads_nodes = (
        send_grads.reshape(experts, capacity, group_size, part_width)
        .transpose(0, 2, 1, 3)
        .reshape(node_count, capacity, part_width)
    )
    got_rows, got_grads = (
        lax.all_to_all(rows_nodes, "node", split_axis=0, concat_axis=0, tiled=True),
        lax.all_to_all(grads_nodes, "node", split_axis=0, concat_axis=0, tiled=True),
    )
    rows_total = node_count * capacity
    got_x = got_rows.reshape(rows_total, feature_width)
    got_h = got_grads.reshape(rows_total, part_width).astype(jnp.float32)
    both_weights = jnp.concatenate([gate_weight, up_weight], axis=1)
    partial_pre = jnp.dot(got_x, both_weights, preferred_element_type=jnp.float32)
    share_width = part_width // local_count
    pre_pairs = partial_pre.reshape(rows_total, 2, part_width)
    own_share = lax.psum_scatter(pre_pairs, "local", scatter_dimension=2, tiled=True)
    first_col = lax.axis_index("local") * share_width
    hidden_share = lax.dynamic_slice_in_dim(got_h, first_col, share_width, 1)
    share_gate, share_up = activate(own_share[:, 0], own_share[:, 1], hidden_share)
    paired = jnp.stack([share_gate, share_up], axis=1)
    gathered = lax.all_gather(paired, "local", axis=2, tiled=True)
    grad_gate = gathered[:, 0]
    grad_up = gathered[:, 1]
    contract_cols = (((1,), (1,)), ((), ()))
    partial_rows = lax.dot_general(
        grad_gate, gate_weight, contract_cols, preferred_element_type=jnp.float32
    )
    partial_rows = partial_rows + lax.dot_general(
        grad_up, up_weight, contract_cols, preferred_element_type=jnp.float32
    )
    partial_rows = partial_rows.astype(jnp.bfloat16).reshape(node_count, capacity, feature_width)
    returned = lax.all_to_all(partial_rows, "node", split_axis=0, concat_axis=0, tiled=True)
    summed = jnp.sum(
        returned.astype(jnp.float32).reshape(experts, group_size, capacity, feature_width), axis=1
    )
    summed = summed.reshape(experts * capacity, feature_width)
    token_grad = jnp.take(summed, slot_of, axis=0).astype(jnp.bfloat16)
    joined = jnp.concatenate([grad_gate, grad_up], axis=1)
    weight_grad = lax.dot_general(
        got_x, joined, (((0,), (0,)), ((), ())), preferred_element_type=jnp.float32
    )
    gate_grad = weight_grad[:, :part_width]
    up_grad = weight_grad[:, part_width:]
    return (token_grad, gate_grad, up_grad)


def solution(mesh):
    in_specs = (
        P("node", "local"),
        P("node"),
        P("node", None),
        P("local", "node"),
        P("local", "node"),
    )
    out_specs = (P("node", "local"), P("local", "node"), P("local", "node"))
    return jax.shard_map(shards, mesh=mesh, in_specs=in_specs, out_specs=out_specs, check_vma=False)
```

profile of v0, /device:TPU:1, one launch (start us, length us, event | category | flops | bytes accessed | tf_op | source)
XLA Modules:
  0.0 232.7 jit_solution(14253780019820898860)
XLA Ops:
  7.2 0.0 copy-start
  7.2 0.8 fusion.12
  8.0 0.2 reduce_window_sum.11
  8.2 0.8 select_reduce_fusion
  9.0 0.7 compare_and_fusion
  9.7 1.1 convolution_convert_fusion.1
  10.8 0.1 broadcast_in_dim.24
  10.8 1.1 broadcast_in_dim.25
  11.9 24.1 %all-to-all-start.1 = ((bf16[64,10,448]{2,1,0:T(8,128)(2,1)}), bf16[64,10,448]{2,1,0:T(8,128)(2,1)S(1)}, u32[]{:S(2)}, u32[]{:S(2)}) async-start(bf16[64,10,448]{2,1,0:T(8,128)(2,1)} %bitcast.2), calls=%async_computation.1 | async-start | bytes 2097152 | tf_op jit(solution)/shard_map/all_to_all | solution.py:47
  36.0 0.0 reduce-scatter.2.cloned.1.call-start
  36.1 0.0 copy-done.2
  36.1 1.1 pad_maximum_fusion
  37.2 26.3 %all-to-all-done.1 = bf16[64,10,448]{2,1,0:T(8,128)(2,1)S(1)} async-done(((bf16[64,10,448]{2,1,0:T(8,128)(2,1)}), bf16[64,10,448]{2,1,0:T(8,128)(2,1)S(1)}, u32[]{:S(2)}, u32[]{:S(2)}) %all-to-all-start.1) | async-done | bytes 573472 | tf_op jit(solution)/shard_map/all_to_all | solution.py:47
  63.5 0.4 reshape.47
  63.9 2.6 %fusion.5 = f32[640,2,512]{0,2,1:T(8,128)} fusion(bf16[56,2,8,512]{3,2,1,0:T(8,128)(2,1)S(1)} %bitcast.50, bf16[640,448]{1,0:T(8,128)(2,1)S(1)} %reshape.47), kind=kOutput, calls=%fused_computation.10 | convolution fusion | flops 587202560 | bytes 4112384 | tf_op jit(solution)/shard_map/dot_general | solution.py:54
  66.4 0.0 reduce-scatter.2.cloned.1.call-update
  66.5 0.0 copy-done
  66.5 0.3 convolution_convert_fusion
  66.8 0.5 reshape.44
  67.3 1.2 copy.25
  68.5 7.7 %all-to-all-start = ((bf16[64,10,512]{2,1,0:T(8,128)(2,1)}), bf16[64,10,512]{2,1,0:T(8,128)(2,1)S(1)}, u32[]{:S(2)}, u32[]{:S(2)}) async-start(bf16[64,10,512]{2,1,0:T(8,128)(2,1)} %bitcast.1), calls=%async_computation | async-start | bytes 2097152 | tf_op jit(solution)/shard_map/all_to_all | solution.py:48
  76.2 0.0 all-gather.2.cloned.1.call-start
  76.3 25.9 %all-to-all-done = bf16[64,10,512]{2,1,0:T(8,128)(2,1)S(1)} async-done(((bf16[64,10,512]{2,1,0:T(8,128)(2,1)}), bf16[64,10,512]{2,1,0:T(8,128)(2,1)S(1)}, u32[]{:S(2)}, u32[]{:S(2)}) %all-to-all-start) | async-done | bytes 655392 | tf_op jit(solution)/shard_map/all_to_all | solution.py:48
  102.1 0.2 reshape.52
  102.3 0.2 constant_dynamic-slice_fusion
  102.5 0.1 copy.28
  102.6 26.4 %reduce-scatter.2.cloned.1.call-done = f32[640,2,32]{0,2,1:T(8,128)} async-done(((f32[640,2,512]{0,2,1:T(8,128)}), f32[640,2,32]{0,2,1:T(8,128)}) %reduce-scatter.2.cloned.1.call-update) | async-done | bytes 163856 | tf_op jit(solution)/shard_map/reduce_scatter | solution.py:57
  129.0 1.0 fusion.16
  130.0 0.0 copy-start.3
  130.0 0.6 pad_maximum_fusion.1
  130.7 0.0 all-gather.2.cloned.1.call-update
  130.7 45.5 %all-gather.2.cloned.1.call-done = bf16[640,2,512]{0,2,1:T(8,128)(2,1)} async-done(((bf16[640,2,32]{0,2,1:T(8,128)(2,1)}), bf16[640,2,512]{0,2,1:T(8,128)(2,1)}) %all-gather.2.cloned.1.call-update) | async-done | bytes 1310736 | tf_op jit(solution)/shard_map/all_gather | solution.py:62
  176.3 1.8 fusion.18
  178.1 0.0 copy-done.3
  178.1 0.0 copy-done.1
  178.1 1.3 fusion
  179.5 1.3 copy.22
  180.8 1.2 reshape.48
  182.0 13.8 %all-to-all-start.2 = ((bf16[64,10,448]{2,1,0:T(8,128)(2,1)}), bf16[64,10,448]{2,1,0:T(8,128)(2,1)S(1)}, u32[]{:S(2)}, u32[]{:S(2)}) async-start(bf16[64,10,448]{2,1,0:T(8,128)(2,1)} %reshape.48), calls=%async_computation.3 | async-start | bytes 2097152 | tf_op jit(solution)/shard_map/all_to_all | solution.py:73
  195.9 0.1 slice_bitcast_fusion.1
  196.0 1.0 fusion.1
  197.0 1.4 fusion.19
  198.4 25.5 %all-to-all-done.2 = bf16[64,10,448]{2,1,0:T(8,128)(2,1)S(1)} async-done(((bf16[64,10,448]{2,1,0:T(8,128)(2,1)}), bf16[64,10,448]{2,1,0:T(8,128)(2,1)S(1)}, u32[]{:S(2)}, u32[]{:S(2)}) %all-to-all-start.2) | async-done | bytes 573472 | tf_op jit(solution)/shard_map/all_to_all | solution.py:73
  223.9 0.2 convert_reduce_fusion
  224.1 0.1 reshape.51
  224.2 0.8 gather_fusion
  225.0 0.1 select_convert_fusion
  225.1 0.8 copy.23
  (4 shorter events, 0.0 us)
Async XLA Ops:
  7.2 59.3 %copy-start = (bf16[128,2048]{1,0:T(8,128)(2,1)S(1)}, bf16[128,2048]{1,0:T(8,128)(2,1)}, u32[]{:S(2)}) copy-start(bf16[128,2048]{1,0:T(8,128)(2,1)} %param.7) | copy-start | bytes 1572868
  11.9 24.1 %copy-start.2 = (bf16[448,512]{1,0:T(8,128)(2,1)S(1)}, bf16[448,512]{1,0:T(8,128)(2,1)}, u32[]{:S(2)}) copy-start(bf16[448,512]{1,0:T(8,128)(2,1)} %param.8) | copy-start | bytes 1376260
  11.9 51.5 %all-to-all-start.1 = ((bf16[64,10,448]{2,1,0:T(8,128)(2,1)}), bf16[64,10,448]{2,1,0:T(8,128)(2,1)S(1)}, u32[]{:S(2)}, u32[]{:S(2)}) async-start(bf16[64,10,448]{2,1,0:T(8,128)(2,1)} %bitcast.2), calls=%async_computation.1 | async-start | bytes 2097152 | tf_op jit(solution)/shard_map/all_to_all | solution.py:47
  36.0 93.0 %reduce-scatter.2.cloned.1.call-start = ((), (), s32[]{:S(2)}) async-start(), calls=%async_computation.4 | async-start | bytes 2785280 | tf_op jit(solution)/shard_map/reduce_scatter | solution.py:57
  68.5 33.6 %all-to-all-start = ((bf16[64,10,512]{2,1,0:T(8,128)(2,1)}), bf16[64,10,512]{2,1,0:T(8,128)(2,1)S(1)}, u32[]{:S(2)}, u32[]{:S(2)}) async-start(bf16[64,10,512]{2,1,0:T(8,128)(2,1)} %bitcast.1), calls=%async_computation | async-start | bytes 2097152 | tf_op jit(solution)/shard_map/all_to_all | solution.py:48
  76.2 100.0 %all-gather.2.cloned.1.call-start = ((), (), s32[]{:S(2)}) async-start(), calls=%async_computation.5 | async-start | bytes 1392640 | tf_op jit(solution)/shard_map/all_gather | solution.py:62
  130.0 48.1 %copy-start.3 = (bf16[448,512]{1,0:T(8,128)(2,1)S(1)}, bf16[448,512]{1,0:T(8,128)(2,1)}, u32[]{:S(2)}) copy-start(bf16[448,512]{1,0:T(8,128)(2,1)} %param.9) | copy-start | bytes 1376260
  176.2 1.9 copy-start.1
  182.0 41.9 %all-to-all-start.2 = ((bf16[64,10,448]{2,1,0:T(8,128)(2,1)}), bf16[64,10,448]{2,1,0:T(8,128)(2,1)S(1)}, u32[]{:S(2)}, u32[]{:S(2)}) async-start(bf16[64,10,448]{2,1,0:T(8,128)(2,1)} %reshape.48), calls=%async_computation.3 | async-start | bytes 2097152 | tf_op jit(solution)/shard_map/all_to_all | solution.py:73
Sparse Core Ops, SparseCore 0:
  66.6 62.4 reduce-scatter.1
  132.3 43.8 all-gather.1
where the time goes:
time: 234 us; the launch traced here: 233 us
  waiting for transfers between devices  150 us (64%)
  starting transfers between devices  45.7 us (20%)
  between operations  14.2 us (6%)
  local copies, waits for them, and re-layouts  9.5 us (4%)
  matrix products  8.15 us (3%)
  other arithmetic  5.51 us (2%)
    all_gather x1, waiting for transfers between devices, shards(): gathered = lax.all_gather(paired, 'local', axis=2, tiled=True)  45.5 us
    reduce_scatter x1, waiting for transfers between devices, shards(): lax.psum_scatter(pre_pairs, 'local', scatter_dimension=2, tiled=True)  26.4 us
    all_to_all x1, waiting for transfers between devices, shards(): lax.all_to_all(rows_nodes, 'node', split_axis=0, concat_axis=0, tiled=True)  26.3 us
    all_to_all x1, waiting for transfers between devices, shards(): lax.all_to_all(grads_nodes, 'node', split_axis=0, concat_axis=0, tiled=True)  25.9 us
    all_to_all x1, waiting for transfers between devices, shards(): lax.all_to_all(partial_rows, 'node', split_axis=0, concat_axis=0, tiled=T...  25.5 us
    all_to_all x1, starting transfers between devices, shards(): lax.all_to_all(rows_nodes, 'node', split_axis=0, concat_axis=0, tiled=True)  24.1 us
    all_to_all x1, starting transfers between devices, shards(): lax.all_to_all(partial_rows, 'node', split_axis=0, concat_axis=0, tiled=T...  13.8 us
    all_to_all x1, starting transfers between devices, shards(): lax.all_to_all(grads_nodes, 'node', split_axis=0, concat_axis=0, tiled=True)  7.72 us
  transfers between devices with their start and end apart: 5, of which 5 were waited for; matrix products, arithmetic and copies ran while one was open for 3% of the time, Pallas kernels for 0%

commit v1 on v0

v1 whole, which is shorter than its diff:
```python
import functools

import jax
import jax.numpy as jnp
from jax import lax
from jax.experimental import pallas as pl
from jax.experimental.pallas import tpu as pltpu
from jax.sharding import PartitionSpec as P

MESH = pl.DeviceIdType.MESH
BF = jnp.bfloat16
F32 = jnp.float32

NZ, NY, NX = 8, 8, 8
GROUP = 4
HALVES = NY // GROUP
CAP = 10
SLOT = 16
FEAT = 448
ROW = 512
HALF = 64
LANE = 128
BLOCK = NZ * CAP
ZROWS = HALVES * SLOT
ZWIDE = ROW + GROUP * HALF
WIDE = NX * LANE
PAIRS = NY // 2
EXPERTS = NZ * HALVES


def iota(shape, dim):
    return lax.broadcasted_iota(jnp.int32, shape, dim)


def dot(a, b, dims=(((1,), (0,)), ((), ()))):
    return lax.dot_general(a, b, dims, preferred_element_type=F32)


def kernel(
    route_ref, tok_ref, hid_ref, gw_ref, uw_ref,
    tg_ref, gg_ref, ug_ref,
    w_ref, zsend, zrecv, ysend, yrecv, sib_out, sib_in, rsum, rsend, rrecv, gath, yout, yret, zout, zret,
    zs_s, zs_r, ys_s, ys_r, sb_s, sb_r, rs_s, rs_r, ag_s, ag_r, rl_s, rl_r, yo_s, yo_r, zo_s, zo_r,
):
    node, local = lax.axis_index("node"), lax.axis_index("local")
    z, y = node // NY, node % NY
    x, c = local // 2, local % 2

    def at_z(d):
        return (((z + d) % NZ) * NY + y, local)

    def at_y(d):
        return (z * NY + (y + d) % NY, local)

    def at_x(d):
        return (node, ((x + d) % NX) * 2 + c)

    sibling = (node, x * 2 + 1 - c)

    def remote(src, dst, s_sem, r_sem, device):
        return pltpu.make_async_remote_copy(
            src_ref=src, dst_ref=dst, send_sem=s_sem, recv_sem=r_sem, device_id=device, device_id_type=MESH
        )

    barrier = pltpu.get_barrier_semaphore()
    for d in range(1, NZ):
        pl.semaphore_signal(barrier, inc=1, device_id=at_z(d), device_id_type=MESH)
    for d in range(1, NY):
        pl.semaphore_signal(barrier, inc=1, device_id=at_y(d), device_id_type=MESH)
    for d in range(1, NX):
        pl.semaphore_signal(barrier, inc=1, device_id=at_x(d), device_id_type=MESH)
    pl.semaphore_signal(barrier, inc=1, device_id=sibling, device_id_type=MESH)

    tok_count = tok_ref.shape[0]
    route = route_ref[...]
    onehot = (iota((EXPERTS, tok_count), 0) == route).astype(F32)
    before = (iota((tok_count, tok_count), 0) < iota((tok_count, tok_count), 1)).astype(BF)
    prior = dot(onehot.astype(BF), before)
    rank = jnp.sum(prior * onehot, axis=0, keepdims=True).astype(jnp.int32)
    slot = route * SLOT + rank
    select = (iota((EXPERTS * SLOT, tok_count), 0) == slot).astype(BF)

    odd = x % 2
    hidden = []
    for g in range(GROUP):
        start = pl.multiple_of(g * (NX * HALF) + (x // 2) * LANE, LANE)
        hidden.append(hid_ref[:, pl.ds(start, LANE)])
    low = iota((LANE, LANE), 0) == iota((LANE, LANE), 1) + HALF * odd
    high = iota((LANE, LANE), 0) == iota((LANE, LANE), 1) - HALF + HALF * odd
    place_low = (low & (iota((LANE, LANE), 1) < HALF)).astype(BF)
    place_high = (high & (iota((LANE, LANE), 1) >= HALF)).astype(BF)

    feat_rows = dot(select, tok_ref[...]).astype(BF)
    hidden_rows = []
    for g in range(0, GROUP, 2):
        both = (dot(hidden[g], place_low) + dot(hidden[g + 1], place_high)).astype(BF)
        hidden_rows.append(dot(select, both).astype(BF))
    for zz in range(NZ):
        rows = slice(zz * ZROWS, (zz + 1) * ZROWS)
        zsend[zz, :, 0:FEAT] = feat_rows[rows]
        zsend[zz, :, FEAT:ROW] = jnp.zeros((ZROWS, ROW - FEAT), BF)
        for i in range(GROUP // 2):
            zsend[zz, :, ROW + i * LANE : ROW + (i + 1) * LANE] = hidden_rows[i][rows]

    pl.semaphore_wait(barrier, (NZ - 1) + (NY - 1) + (NX - 1) + 1)

    def z_copy(d):
        return remote(zsend.at[(z + d) % NZ], zrecv.at[z], zs_s.at[d], zs_r.at[d], at_z(d))

    for d in range(1, NZ):
        z_copy(d).start()
    zrecv[z] = zsend[z]

    for i in range(NX // 2):
        g_part = gw_ref[:, i * LANE : (i + 1) * LANE]
        u_part = uw_ref[:, i * LANE : (i + 1) * LANE]
        w_ref[0:FEAT, 2 * i * LANE : (2 * i + 1) * LANE] = jnp.concatenate([g_part[:, :HALF], u_part[:, :HALF]], axis=1)
        w_ref[0:FEAT, (2 * i + 1) * LANE : (2 * i + 2) * LANE] = jnp.concatenate([g_part[:, HALF:], u_part[:, HALF:]], axis=1)
    w_ref[FEAT:ROW, :] = jnp.zeros((ROW - FEAT, WIDE), BF)

    out_i = iota((HALVES * BLOCK, NZ * ZROWS), 0)
    in_i = iota((HALVES * BLOCK, NZ * ZROWS), 1)
    out_h = out_i // BLOCK
    out_z = (out_i % BLOCK) // CAP
    compact = (in_i == out_z * ZROWS + out_h * SLOT + out_i % CAP).astype(BF)

    for d in range(1, NZ):
        z_copy(d).wait_recv()
    rows_in = zrecv[...].reshape(NZ * ZROWS, ZWIDE)
    packed = dot(compact, rows_in).astype(BF)
    for h in range(HALVES):
        part = packed[h * BLOCK : (h + 1) * BLOCK]
        for g in range(GROUP):
            ysend[h * GROUP + g, :, 0 : ROW - LANE] = part[:, 0 : ROW - LANE]
            ysend[h * GROUP + g, :, ROW - LANE : ROW] = jnp.concatenate(
                [part[:, ROW - LANE : FEAT], part[:, ROW + g * HALF : ROW + (g + 1) * HALF]], axis=1
            )

    def y_copy(d):
        return remote(ysend.at[(y + d) % NY], yrecv.at[NY - d], ys_s.at[d], ys_r.at[d], at_y(d))

    for d in (7, 1, 6, 2, 5, 3, 4):
        y_copy(d).start()
    yrecv[0] = ysend[y]

    def slots(p):
        a, b = (NY - p) % NY, p + 1
        return ((1 - c) * a + c * b) % NY, (c * a + (1 - c) * b) % NY

    def sib_copy(p):
        return remote(sib_out.at[p], sib_in.at[p], sb_s.at[p], sb_r.at[p], sibling)

    def rs_copy(p, d):
        return remote(rsend.at[p, (x + d) % NX], rrecv.at[p, d], rs_s.at[p, d], rs_r.at[p, d], at_x(d))

    def ag_copy(p, d):
        mine, _ = slots(p)
        return remote(gath.at[mine, x], gath.at[mine, x], ag_s.at[p, d], ag_r.at[p, d], at_x(d))

    def relay_copy(p, d):
        mine, _ = slots(p)
        chip = (x + NX - d) % NX
        return remote(gath.at[mine, chip], gath.at[mine, chip], rl_s.at[p, d], rl_r.at[p, d], sibling)

    def yo_copy(k):
        return remote(yout.at[k], yret.at[y], yo_s.at[k], yo_r.at[k], at_y(k))

    def reduce_out(p):
        a, b = (NY - p) % NY, p + 1
        for k in (a, b):
            if k:
                y_copy(NY - k).wait_recv()
        mine, other = slots(p)
        pair = jnp.concatenate([yrecv[other], yrecv[mine]], axis=0)
        pre = dot(pair, w_ref[...])
        sib_out[p] = pre[:BLOCK]
        sib_copy(p).start()
        sib_copy(p).wait_recv()
        total = pre[BLOCK:] + sib_in[p]
        for i in range(NX):
            part = total[:, i * LANE : (i + 1) * LANE]
            rsum[p, i] = part
            rsend[p, i] = part.astype(BF)
        for d in range(1, NX):
            rs_copy(p, d).start()

    def activate_share(p):
        for d in range(1, NX):
            rs_copy(p, d).wait_recv()
        mine, _ = slots(p)
        pre = rsum[p, x]
        for d in range(1, NX):
            pre = pre + rrecv[p, d].astype(F32)
        gate_pre, up_pre = pre[:, :HALF], pre[:, HALF:]
        hidden_part = yrecv[mine, :, ROW - LANE : ROW].astype(F32)[:, HALF:]
        s = 1.0 / (1.0 + jnp.exp(-gate_pre))
        grad_up = hidden_part * (gate_pre * s)
        grad_gate = hidden_part * up_pre * (s * (1.0 + gate_pre * (1.0 - s)))
        gath[mine, x] = jnp.concatenate([grad_gate, grad_up], axis=1).astype(BF)
        relay_copy(p, 0).start()
        for d in range(1, NX):
            ag_copy(p, d).start()

    def rows_back(p):
        for d in range(1, NX):
            ag_copy(p, d).wait_recv()
            relay_copy(p, d).start()
        for d in range(NX):
            relay_copy(p, d).wait_recv()
        a, b = (NY - p) % NY, p + 1
        both = [jnp.concatenate([gath[k, i] for i in range(NX)], axis=1) for k in (a, b)]
        back = dot(jnp.concatenate(both, axis=0), w_ref[...], (((1,), (1,)), ((), ()))).astype(BF)
        for i, k in enumerate((a, b)):
            if k:
                yout[k] = back[i * BLOCK : (i + 1) * BLOCK]
                yo_copy(k).start()
            else:
                yret[y] = back[i * BLOCK : (i + 1) * BLOCK]

    reduce_out(0)
    reduce_out(1)
    activate_share(0)
    reduce_out(2)
    activate_share(1)
    reduce_out(3)
    activate_share(2)
    rows_back(0)
    activate_share(3)
    rows_back(1)
    rows_back(2)
    rows_back(3)

    rows_x = yrecv[...].reshape(NY * BLOCK, ROW)
    for i in range(NX // 2):
        pair = jnp.concatenate([gath[:, 2 * i].reshape(NY * BLOCK, LANE), gath[:, 2 * i + 1].reshape(NY * BLOCK, LANE)], axis=1)
        both = dot(rows_x, pair, (((0,), (0,)), ((), ())))[:FEAT]
        first, second = both[:, :LANE], both[:, LANE:]
        gg_ref[:, i * LANE : (i + 1) * LANE] = jnp.concatenate([first[:, :HALF], second[:, :HALF]], axis=1)
        ug_ref[:, i * LANE : (i + 1) * LANE] = jnp.concatenate([first[:, HALF:], second[:, HALF:]], axis=1)

    for k in range(1, NY):
        yo_copy(k).wait_recv()
    sums = []
    for h in range(HALVES):
        acc = yret[h * GROUP].astype(F32)
        for g in range(1, GROUP):
            acc = acc + yret[h * GROUP + g].astype(F32)
        sums.append(acc.astype(BF))
    spread_i = iota((NZ * ZROWS, HALVES * BLOCK), 0)
    from_i = iota((NZ * ZROWS, HALVES * BLOCK), 1)
    spread_r = spread_i % SLOT
    spread_h = (spread_i % ZROWS) // SLOT
    spread = (
        (from_i == spread_h * BLOCK + (spread_i // ZROWS) * CAP + spread_r) & (spread_r < CAP)
    ).astype(BF)
    back_rows = dot(spread, jnp.concatenate(sums, axis=0)).astype(BF)
    for zz in range(NZ):
        zout[zz] = back_rows[zz * ZROWS : (zz + 1) * ZROWS]

    def zo_copy(d):
        return remote(zout.at[(z + d) % NZ], zret.at[z], zo_s.at[d], zo_r.at[d], at_z(d))

    for d in range(1, NZ):
        zo_copy(d).start()
    zret[z] = zout[z]
    for d in range(1, NZ):
        zo_copy(d).wait_recv()
    got = zret[...].reshape(NZ * ZROWS, ROW)
    mine_back = dot(select, got, (((0,), (0,)), ((), ())))
    tg_ref[...] = mine_back[:, :FEAT].astype(BF)

    for d in range(1, NZ):
        z_copy(d).wait_send()
        zo_copy(d).wait_send()
    for d in range(1, NY):
        y_copy(d).wait_send()
        yo_copy(d).wait_send()
    for p in range(PAIRS):
        sib_copy(p).wait_send()
        relay_copy(p, 0).wait_send()
        for d in range(1, NX):
            rs_copy(p, d).wait_send()
            ag_copy(p, d).wait_send()
            relay_copy(p, d).wait_send()


def shards(tokens, route_expert, hidden_grad, gate_weight, up_weight):
    vmem = pl.BlockSpec(memory_space=pltpu.VMEM)
    dma = pltpu.SemaphoreType.DMA
    return pl.pallas_call(
        kernel,
        out_shape=(
            jax.ShapeDtypeStruct(tokens.shape, BF),
            jax.ShapeDtypeStruct(gate_weight.shape, F32),
            jax.ShapeDtypeStruct(up_weight.shape, F32),
        ),
        in_specs=[vmem] * 5,
        out_specs=(vmem, vmem, vmem),
        scratch_shapes=[
            pltpu.VMEM((ROW, WIDE), BF),
            pltpu.VMEM((NZ, ZROWS, ZWIDE), BF),
            pltpu.VMEM((NZ, ZROWS, ZWIDE), BF),
            pltpu.VMEM((NY, BLOCK, ROW), BF),
            pltpu.VMEM((NY, BLOCK, ROW), BF),
            pltpu.VMEM((PAIRS, BLOCK, WIDE), F32),
            pltpu.VMEM((PAIRS, BLOCK, WIDE), F32),
            pltpu.VMEM((PAIRS, NX, BLOCK, LANE), F32),
            pltpu.VMEM((PAIRS, NX, BLOCK, LANE), BF),
            pltpu.VMEM((PAIRS, NX, BLOCK, LANE), BF),
            pltpu.VMEM((NY, NX, BLOCK, LANE), BF),
            pltpu.VMEM((NY, BLOCK, ROW), BF),
            pltpu.VMEM((NY, BLOCK, ROW), BF),
            pltpu.VMEM((NZ, ZROWS, ROW), BF),
            pltpu.VMEM((NZ, ZROWS, ROW), BF),
            dma((NZ,)), dma((NZ,)),
            dma((NY,)), dma((NY,)),
            dma((PAIRS,)), dma((PAIRS,)),
            dma((PAIRS, NX)), dma((PAIRS, NX)),
            dma((PAIRS, NX)), dma((PAIRS, NX)),
            dma((PAIRS, NX)), dma((PAIRS, NX)),
            dma((NY,)), dma((NY,)),
            dma((NZ,)), dma((NZ,)),
        ],
        compiler_params=pltpu.CompilerParams(
            collective_id=0, has_side_effects=True, vmem_limit_bytes=56 * 1024 * 1024
        ),
    )(route_expert.reshape(1, -1), tokens, hidden_grad, gate_weight, up_weight)


def solution(mesh):
    in_specs = (
        P("node", "local"),
        P("node"),
        P("node", None),
        P("local", "node"),
        P("local", "node"),
    )
    out_specs = (P("node", "local"), P("local", "node"), P("local", "node"))
    return jax.shard_map(shards, mesh=mesh, in_specs=in_specs, out_specs=out_specs, check_vma=False)
```

time: 234 us -> 107 us (0.46)
  waiting for transfers between devices: 150 us -> 0 us
  Pallas kernels: 0 us -> 98.4 us
  starting transfers between devices: 45.7 us -> 0 us
  between operations: 14.2 us -> 0.64 us
  matrix products: 8.15 us -> 0 us
  other arithmetic: 5.51 us -> 0 us
  local copies, waits for them, and re-layouts: 9.5 us -> 6.5 us
    pallas_call x0 -> x1, Pallas kernels: none -> 98.4 us  [shards(): pl.pallas_call(kernel, out_shape=(jax.ShapeDtypeStruct(tokens.shape, BF),...]
    all_to_all x3 -> x0, waiting for transfers between devices: 77.6 us -> none  [the longest x1 26.3 us: shards(): lax.all_to_all(rows_nodes, 'node', split_axis=0, concat_axis=0, tiled=True)]
    all_to_all x3 -> x0, starting transfers between devices: 45.6 us -> none  [the longest x1 24.1 us: shards(): lax.all_to_all(rows_nodes, 'node', split_axis=0, concat_axis=0, tiled=True)]
    all_gather x1 -> x0, waiting for transfers between devices: 45.5 us -> none  [shards(): gathered = lax.all_gather(paired, 'local', axis=2, tiled=True)]
    reduce_scatter x1 -> x0, waiting for transfers between devices: 26.4 us -> none  [shards(): lax.psum_scatter(pre_pairs, 'local', scatter_dimension=2, tiled=True)]
    dot_general x6 -> x0, matrix products: 8.15 us -> none  [the longest x1 2.55 us: shards(): jnp.dot(got_x, both_weights, preferred_element_type=jnp.float32)]
    unnamed x10 -> x5, local copies, waits for them, and re-layouts: 0.92 us -> 4.83 us
    reshape x5 -> x0, local copies, waits for them, and re-layouts: 3.41 us -> none  [the longest x1 1.24 us: shards(): partial_rows.astype(jnp.bfloat16)]
  transfers between devices with their start and end apart: 5 -> 0, of which waited for: 5 -> 0; matrix products, arithmetic and copies ran while one was open for 3% -> 0% of each run, Pallas kernels for 0% -> 0%
where the time goes in v1:
time: 107 us; the launch traced here: 106 us
  Pallas kernels  98.4 us (92%)
  local copies, waits for them, and re-layouts  6.5 us (6%)
    pallas_call x1, Pallas kernels, shards(): pl.pallas_call(kernel, out_shape=(jax.ShapeDtypeStruct(tokens.shape, BF),...  98.4 us
    unnamed x5, local copies, waits for them, and re-layouts  4.83 us

profile of v1, /device:TPU:1, one launch (start us, length us, event | category | flops | bytes accessed | tf_op | source)
XLA Modules:
  0.0 105.6 jit_solution(3882059496001190918)
XLA Ops:
  0.6 1.7 %copy.8.tok_ref = bf16[128,448]{1,0:T(8,128)(2,1)} copy(bf16[128,448]{0,1:T(8,128)(2,1)} %param.5) | data formatting | bytes 229376 | tf_op args[0]
  2.3 98.4 %shard_map.76 = (bf16[128,448]{1,0:T(8,128)(2,1)}, f32[448,512]{1,0:T(8,128)}, f32[448,512]{1,0:T(8,128)}) custom-call(s32[1,128]{1,0:T(1,128)} %bitcast.1, bf16[128,448]{1,0:T(8,128)(2,1)} %copy.8.tok_ref, bf16[128,2048]{1,0:T(8,128)(2,1)} %hid_ref.1, bf16[448,512]{1,0:T(8,128)(2,1)} %gw_ref.1, bf16[448,512]{1,0:T(8,128)(2,1)} %uw_ref.1), custom_call_target="tpu_custom_call" | custom-call | tf_op jit(solution)/shard_map/pallas_call | solution.py:290
  100.7 1.7 %copy.9 = bf16[128,448]{0,1:T(8,128)(2,1)} copy(bf16[128,448]{1,0:T(8,128)(2,1)} %get-tuple-element.3) | data formatting | bytes 229376 | tf_op jit(solution)/shard_map/pallas_call | solution.py:290
  102.4 0.0 copy-start
  102.4 2.2 %copy.12 = f32[448,512]{1,0:T(8,128)} copy(f32[448,512]{1,0:T(8,128)} %get-tuple-element.10) | data formatting | bytes 1835008
  104.6 0.0 copy-done
  104.6 0.9 copy.13
Async XLA Ops:
  102.4 2.2 %copy-start = (f32[448,512]{1,0:T(8,128)S(1)}, f32[448,512]{1,0:T(8,128)}, u32[]{:S(2)}) copy-start(f32[448,512]{1,0:T(8,128)} %get-tuple-element.11) | copy-start | bytes 2752516

commit v2 on v1

v2 whole, which is shorter than its diff:
```python
import functools

import jax
import jax.numpy as jnp
from jax import lax
from jax.experimental import pallas as pl
from jax.experimental.pallas import tpu as pltpu
from jax.sharding import PartitionSpec as P

MESH = pl.DeviceIdType.MESH
BF = jnp.bfloat16
F32 = jnp.float32

NZ, NY, NX = 8, 8, 8
GROUP = 4
HALVES = NY // GROUP
CAP = 10
FEAT = 448
ROW = 512
HALF = 64
LANE = 128
BLOCK = NZ * CAP
SHARE = HALVES * CAP
IN_ROWS = 112
OUT_ROWS = 4 * SHARE
WIDE = NX * LANE
PAIR = ((0, 4), (5, 3), (6, 2), (7, 1))
PAIRS = len(PAIR)
EXPERTS = NZ * HALVES


def iota(shape, dim):
    return lax.broadcasted_iota(jnp.int32, shape, dim)


def dot(a, b, dims=(((1,), (0,)), ((), ()))):
    return lax.dot_general(a, b, dims, preferred_element_type=F32)


def kernel(
    route_any, tok_any, hid_any, gw_any, uw_any,
    tg_ref, gg_any, ug_any,
    route_ref, tok_ref, hid_ref, gw_ref, uw_ref, gg_ref, ug_ref, compact, spread, pick,
    w_ref, zsend, zrecv, ysend, yrecv, sib_out, sib_in, rsum, rsend, rrecv, gath, yout, yret, zout, zret, in_s,
    zs_s, zs_r, ys_s, ys_r, sb_s, sb_r, rs_s, rs_r, ag_s, ag_r, rl_s, rl_r, yo_s, yo_r, zo_s, zo_r,
):
    node, local = lax.axis_index("node"), lax.axis_index("local")
    z, y = node // NY, node % NY
    x, c = local // 2, local % 2

    def at_z(d):
        return (((z + d) % NZ) * NY + y, local)

    def at_y(d):
        return (z * NY + (y + d) % NY, local)

    def at_x(d):
        return (node, ((x + d) % NX) * 2 + c)

    sibling = (node, x * 2 + 1 - c)

    def remote(src, dst, s_sem, r_sem, device):
        return pltpu.make_async_remote_copy(
            src_ref=src, dst_ref=dst, send_sem=s_sem, recv_sem=r_sem, device_id=device, device_id_type=MESH
        )

    odd = x % 2
    loads = [
        pltpu.make_async_copy(route_any, route_ref, in_s.at[0]),
        pltpu.make_async_copy(tok_any, tok_ref.at[0:FEAT], in_s.at[1]),
        pltpu.make_async_copy(gw_any, gw_ref, in_s.at[2]),
        pltpu.make_async_copy(uw_any, uw_ref, in_s.at[3]),
    ]
    for g in range(GROUP):
        start = pl.multiple_of(g * (NX * HALF) + (x // 2) * LANE, LANE)
        loads.append(pltpu.make_async_copy(hid_any.at[:, pl.ds(start, LANE)], hid_ref.at[g], in_s.at[4 + g]))
    for i in (0, 1, 4, 5, 6, 7, 2, 3):
        loads[i].start()

    barrier = pltpu.get_barrier_semaphore()
    for d in range(1, NZ):
        pl.semaphore_signal(barrier, inc=1, device_id=at_z(d), device_id_type=MESH)
    for d in range(1, NY):
        pl.semaphore_signal(barrier, inc=1, device_id=at_y(d), device_id_type=MESH)
    for d in range(1, NX):
        pl.semaphore_signal(barrier, inc=1, device_id=at_x(d), device_id_type=MESH)
    pl.semaphore_signal(barrier, inc=1, device_id=sibling, device_id_type=MESH)

    tok_count = tok_ref.shape[1]
    tok_ref[FEAT:ROW, :] = jnp.zeros((ROW - FEAT, tok_count), BF)
    before = (iota((tok_count, tok_count), 0) < iota((tok_count, tok_count), 1)).astype(BF)
    lane = iota((LANE, LANE), 1)
    shifted = iota((LANE, LANE), 0) - HALF * odd
    place_low = ((shifted == lane) & (lane < HALF)).astype(BF)
    place_high = ((shifted == lane - HALF) & (lane >= HALF)).astype(BF)
    loads[0].wait()
    route = route_ref[...]
    onehot = (iota((EXPERTS, tok_count), 0) == route).astype(F32)
    prior = dot(onehot.astype(BF), before)
    rank = jnp.sum(prior * onehot, axis=0, keepdims=True).astype(jnp.int32)
    to_z, to_h = route // HALVES, route % HALVES
    in_row = iota((NZ * IN_ROWS, tok_count), 0)
    first = to_z * IN_ROWS + to_h * CAP + rank
    last = to_z * IN_ROWS + 5 * SHARE + rank

    loads[1].wait()
    by_lane = (((1,), (1,)), ((), ()))
    packed = jnp.zeros((NZ * IN_ROWS, LANE), F32)
    for j in range(4):
        packed = packed + dot((in_row == first + j * SHARE).astype(BF), tok_ref[j * LANE : (j + 1) * LANE, :], by_lane)
    for g in range(GROUP):
        loads[4 + g].wait()
    hidden_0 = dot(hid_ref[0], place_high).astype(BF)
    hidden_12 = (dot(hid_ref[1], place_low) + dot(hid_ref[2], place_high)).astype(BF)
    hidden_3 = [dot(hid_ref[3], place).astype(BF) for place in (place_low, place_high)]
    packed = packed + dot((in_row == first + 3 * SHARE).astype(BF), hidden_0)
    packed = packed + dot((in_row == first + 4 * SHARE).astype(BF), hidden_12)
    for h in range(HALVES):
        packed = packed + dot(((in_row == last) & (to_h == h)).astype(BF), hidden_3[h])
    for zz in range(NZ):
        zsend[zz] = packed[zz * IN_ROWS : (zz + 1) * IN_ROWS].astype(BF)

    pl.semaphore_wait(barrier, (NZ - 1) + (NY - 1) + (NX - 1) + 1)

    def z_copy(d):
        return remote(zsend.at[(z + d) % NZ], zrecv.at[z], zs_s.at[d], zs_r.at[d], at_z(d))

    for d in range(1, NZ):
        z_copy(d).start()
    zrecv[z] = zsend[z]

    loads[2].wait()
    loads[3].wait()
    for i in range(NX // 2):
        g_part = gw_ref[:, i * LANE : (i + 1) * LANE]
        u_part = uw_ref[:, i * LANE : (i + 1) * LANE]
        w_ref[0:FEAT, 2 * i * LANE : (2 * i + 1) * LANE] = jnp.concatenate([g_part[:, :HALF], u_part[:, :HALF]], axis=1)
        w_ref[0:FEAT, (2 * i + 1) * LANE : (2 * i + 2) * LANE] = jnp.concatenate([g_part[:, HALF:], u_part[:, HALF:]], axis=1)
    w_ref[FEAT:ROW, :] = jnp.zeros((ROW - FEAT, WIDE), BF)

    out_i = iota((HALVES * BLOCK, NZ * IN_ROWS), 0)
    in_i = iota((HALVES * BLOCK, NZ * IN_ROWS), 1)
    start = ((out_i % BLOCK) // CAP) * IN_ROWS + out_i % CAP
    for j in range(5):
        compact[j] = (in_i == start + (out_i // BLOCK) * CAP + j * SHARE).astype(BF)
    compact[5] = (in_i == start + 5 * SHARE).astype(BF)

    out_i = iota((NZ * OUT_ROWS, HALVES * BLOCK), 0)
    in_i = iota((NZ * OUT_ROWS, HALVES * BLOCK), 1)
    start = ((in_i % BLOCK) // CAP) * OUT_ROWS + (in_i // BLOCK) * CAP + in_i % CAP
    out_row = iota((NZ * OUT_ROWS, tok_count), 0)
    for j in range(4):
        spread[j] = (out_i == start + j * SHARE).astype(BF)
        pick[:, j * LANE : (j + 1) * LANE] = (out_row == to_z * OUT_ROWS + to_h * CAP + rank + j * SHARE).astype(BF)

    for d in range(1, NZ):
        z_copy(d).wait_recv()
    rows_in = zrecv[...].reshape(NZ * IN_ROWS, LANE)
    parts = [dot(compact[j], rows_in).astype(BF) for j in range(6)]
    for h in range(HALVES):
        rows = slice(h * BLOCK, (h + 1) * BLOCK)
        features, mixed, middle, final = parts[:3], parts[3][rows], parts[4][rows], parts[5][rows]
        for g in range(GROUP):
            for j in range(3):
                ysend[h * GROUP + g, :, j * LANE : (j + 1) * LANE] = features[j][rows]
            hidden = (mixed[:, HALF:], middle[:, :HALF], middle[:, HALF:], final[:, h * HALF : (h + 1) * HALF])[g]
            ysend[h * GROUP + g, :, ROW - LANE : ROW] = jnp.concatenate([mixed[:, :HALF], hidden], axis=1)

    def y_copy(d):
        return remote(ysend.at[(y + d) % NY], yrecv.at[NY - d], ys_s.at[d], ys_r.at[d], at_y(d))

    y_copy(4).start()
    yrecv[0] = ysend[y]
    y_copy(4).wait_send()
    y_copy(3).start()
    y_copy(5).start()

    def slots(p):
        a, b = PAIR[p]
        return ((1 - c) * a + c * b) % NY, (c * a + (1 - c) * b) % NY

    def sib_copy(p):
        return remote(sib_out.at[p], sib_in.at[p], sb_s.at[p], sb_r.at[p], sibling)

    def rs_copy(p, d):
        return remote(rsend.at[p, (x + d) % NX], rrecv.at[p, d], rs_s.at[p, d], rs_r.at[p, d], at_x(d))

    def ag_copy(p, d):
        mine, _ = slots(p)
        return remote(gath.at[mine, x], gath.at[mine, x], ag_s.at[p, d], ag_r.at[p, d], at_x(d))

    def relay_copy(p, d):
        mine, _ = slots(p)
        chip = (x + NX - d) % NX
        return remote(gath.at[mine, chip], gath.at[mine, chip], rl_s.at[p, d], rl_r.at[p, d], sibling)

    def yo_copy(k):
        return remote(yout.at[k], yret.at[y], yo_s.at[k], yo_r.at[k], at_y(k))

    def next_sends(done, d):
        for k in (done, NY - done):
            y_copy(k).wait_send()
        for k in (d, NY - d):
            y_copy(k).start()

    def pre_part(p):
        for k in PAIR[p]:
            if k:
                y_copy(NY - k).wait_recv()
        mine, other = slots(p)
        pair = jnp.concatenate([yrecv[other], yrecv[mine]], axis=0)
        pre = dot(pair, w_ref[...])
        sib_out[p] = pre[:BLOCK]
        sib_copy(p).start()
        for i in range(NX):
            rsum[p, i] = pre[BLOCK:, i * LANE : (i + 1) * LANE]

    def reduce_near(p):
        sib_copy(p).wait_recv()
        for i in range(NX):
            part = rsum[p, i] + sib_in[p, :, i * LANE : (i + 1) * LANE]
            rsum[p, i] = part
            rsend[p, i] = part.astype(BF)
        for d in range(1, NX):
            rs_copy(p, d).start()

    def rs_wait(p):
        for d in range(1, NX):
            rs_copy(p, d).wait_recv()

    def activate_share(p):
        rs_wait(p)
        mine, _ = slots(p)
        pre = rsum[p, x]
        for d in range(1, NX):
            pre = pre + rrecv[p, d].astype(F32)
        gate_pre, up_pre = pre[:, :HALF], pre[:, HALF:]
        hidden_part = yrecv[mine, :, ROW - LANE : ROW].astype(F32)[:, HALF:]
        s = 1.0 / (1.0 + jnp.exp(-gate_pre))
        grad_up = hidden_part * (gate_pre * s)
        grad_gate = hidden_part * up_pre * (s * (1.0 + gate_pre * (1.0 - s)))
        gath[mine, x] = jnp.concatenate([grad_gate, grad_up], axis=1).astype(BF)
        relay_copy(p, 0).start()
        for d in range(1, NX):
            ag_copy(p, d).start()

    def gather_share(p):
        for d in (1, 7, 2, 6, 3, 5, 4):
            ag_copy(p, d).wait_recv()
            relay_copy(p, d).start()

    def gather_wait(p):
        for d in range(NX):
            relay_copy(p, d).wait_recv()

    def rows_back(p):
        gather_wait(p)
        a, b = PAIR[p]
        both = [jnp.concatenate([gath[k, i] for i in range(NX)], axis=1) for k in (a, b)]
        back = dot(jnp.concatenate(both, axis=0), w_ref[...], (((1,), (1,)), ((), ()))).astype(BF)
        for i, k in enumerate((a, b)):
            if k:
                yout[k] = back[i * BLOCK : (i + 1) * BLOCK]
                yo_copy(k).start()
            else:
                yret[y] = back[i * BLOCK : (i + 1) * BLOCK]

    pre_part(0)
    reduce_near(0)
    next_sends(3, 2)
    pre_part(1)
    reduce_near(1)
    activate_share(0)
    next_sends(2, 1)
    pre_part(2)
    reduce_near(2)
    pre_part(3)
    activate_share(1)
    gather_share(0)
    reduce_near(3)
    rows_back(0)
    activate_share(2)
    gather_share(1)
    activate_share(3)
    rows_back(1)
    gather_share(2)
    rows_back(2)
    gather_share(3)
    rows_back(3)

    for k in range(1, NY):
        yo_copy(k).wait_recv()
    sums = []
    for h in range(HALVES):
        acc = yret[h * GROUP].astype(F32)
        for g in range(1, GROUP):
            acc = acc + yret[h * GROUP + g].astype(F32)
        sums.append(acc.astype(BF))
    total = jnp.concatenate(sums, axis=0)
    back_rows = dot(spread[0], total[:, :LANE])
    for j in range(1, 4):
        back_rows = back_rows + dot(spread[j], total[:, j * LANE : (j + 1) * LANE])
    for zz in range(NZ):
        zout[zz] = back_rows[zz * OUT_ROWS : (zz + 1) * OUT_ROWS].astype(BF)

    def zo_copy(d):
        return remote(zout.at[(z + d) % NZ], zret.at[z], zo_s.at[d], zo_r.at[d], at_z(d))

    for d in range(1, NZ):
        zo_copy(d).start()
    zret[z] = zout[z]

    rows_x = yrecv[...].reshape(NY * BLOCK, ROW)
    for i in range(NX // 2):
        pair = jnp.concatenate([gath[:, 2 * i].reshape(NY * BLOCK, LANE), gath[:, 2 * i + 1].reshape(NY * BLOCK, LANE)], axis=1)
        both = dot(rows_x, pair, (((0,), (0,)), ((), ())))[:FEAT]
        first, second = both[:, :LANE], both[:, LANE:]
        gg_ref[:, i * LANE : (i + 1) * LANE] = jnp.concatenate([first[:, :HALF], second[:, :HALF]], axis=1)
        ug_ref[:, i * LANE : (i + 1) * LANE] = jnp.concatenate([first[:, HALF:], second[:, HALF:]], axis=1)
    stores = [
        pltpu.make_async_copy(gg_ref, gg_any, in_s.at[0]),
        pltpu.make_async_copy(ug_ref, ug_any, in_s.at[1]),
    ]
    for store in stores:
        store.start()

    for d in range(1, NZ):
        zo_copy(d).wait_recv()
    got = zret[...].reshape(NZ * OUT_ROWS, LANE)
    mine_back = dot(got, pick[...], (((0,), (0,)), ((), ()))).astype(BF)
    for j in range(4):
        rows = min(LANE, FEAT - j * LANE)
        tg_ref[j * LANE : j * LANE + rows, :] = mine_back[:rows, j * LANE : (j + 1) * LANE]

    for store in stores:
        store.wait()
    for d in range(1, NZ):
        z_copy(d).wait_send()
        zo_copy(d).wait_send()
    y_copy(1).wait_send()
    y_copy(7).wait_send()
    for d in range(1, NY):
        yo_copy(d).wait_send()
    for p in range(PAIRS):
        sib_copy(p).wait_send()
        relay_copy(p, 0).wait_send()
        for d in range(1, NX):
            rs_copy(p, d).wait_send()
            ag_copy(p, d).wait_send()
            relay_copy(p, d).wait_send()


def shards(tokens, route_expert, hidden_grad, gate_weight, up_weight):
    vmem, anywhere = pl.BlockSpec(memory_space=pltpu.VMEM), pl.BlockSpec(memory_space=pl.ANY)
    tok_count = tokens.shape[0]
    dma = pltpu.SemaphoreType.DMA
    token_grad, gate_grad, up_grad = pl.pallas_call(
        kernel,
        out_shape=(
            jax.ShapeDtypeStruct(tokens.shape[::-1], BF),
            jax.ShapeDtypeStruct(gate_weight.shape, F32),
            jax.ShapeDtypeStruct(up_weight.shape, F32),
        ),
        in_specs=[anywhere] * 5,
        out_specs=(vmem, anywhere, anywhere),
        scratch_shapes=[
            pltpu.VMEM((1, tok_count), jnp.int32),
            pltpu.VMEM((ROW, tok_count), BF),
            pltpu.VMEM((GROUP, tok_count, LANE), BF),
            pltpu.VMEM(gate_weight.shape, BF),
            pltpu.VMEM(up_weight.shape, BF),
            pltpu.VMEM(gate_weight.shape, F32),
            pltpu.VMEM(up_weight.shape, F32),
            pltpu.VMEM((6, HALVES * BLOCK, NZ * IN_ROWS), BF),
            pltpu.VMEM((4, NZ * OUT_ROWS, HALVES * BLOCK), BF),
            pltpu.VMEM((NZ * OUT_ROWS, 4 * tok_count), BF),
            pltpu.VMEM((ROW, WIDE), BF),
            pltpu.VMEM((NZ, IN_ROWS, LANE), BF),
            pltpu.VMEM((NZ, IN_ROWS, LANE), BF),
            pltpu.VMEM((NY, BLOCK, ROW), BF),
            pltpu.VMEM((NY, BLOCK, ROW), BF),
            pltpu.VMEM((PAIRS, BLOCK, WIDE), F32),
            pltpu.VMEM((PAIRS, BLOCK, WIDE), F32),
            pltpu.VMEM((PAIRS, NX, BLOCK, LANE), F32),
            pltpu.VMEM((PAIRS, NX, BLOCK, LANE), BF),
            pltpu.VMEM((PAIRS, NX, BLOCK, LANE), BF),
            pltpu.VMEM((NY, NX, BLOCK, LANE), BF),
            pltpu.VMEM((NY, BLOCK, ROW), BF),
            pltpu.VMEM((NY, BLOCK, ROW), BF),
            pltpu.VMEM((NZ, OUT_ROWS, LANE), BF),
            pltpu.VMEM((NZ, OUT_ROWS, LANE), BF),
            dma((8,)),
            dma((NZ,)), dma((NZ,)),
            dma((NY,)), dma((NY,)),
            dma((PAIRS,)), dma((PAIRS,)),
            dma((PAIRS, NX)), dma((PAIRS, NX)),
            dma((PAIRS, NX)), dma((PAIRS, NX)),
            dma((PAIRS, NX)), dma((PAIRS, NX)),
            dma((NY,)), dma((NY,)),
            dma((NZ,)), dma((NZ,)),
        ],
        compiler_params=pltpu.CompilerParams(
            collective_id=0, has_side_effects=True, vmem_limit_bytes=56 * 1024 * 1024
        ),
    )(route_expert.reshape(1, -1), tokens.T, hidden_grad, gate_weight, up_weight)
    return token_grad.T, gate_grad, up_grad


def solution(mesh):
    in_specs = (
        P("node", "local"),
        P("node"),
        P("node", None),
        P("local", "node"),
        P("local", "node"),
    )
    out_specs = (P("node", "local"), P("local", "node"), P("local", "node"))
    return jax.shard_map(shards, mesh=mesh, in_specs=in_specs, out_specs=out_specs, check_vma=False)
```

time: 107 us -> 95.5 us (0.89); the launches traced: 106 us -> 95.2 us
  Pallas kernels: 98.4 us -> 89.9 us
  local copies, waits for them, and re-layouts: 6.5 us -> 4.72 us
    pallas_call x1, Pallas kernels: 98.4 us -> 89.9 us  [shards(): pl.pallas_call(kernel, out_shape=(jax.ShapeDtypeStruct(tokens.shape[::-1]...]
    pallas_call x1 -> x0, local copies, waits for them, and re-layouts: 1.67 us -> none  [shards(): pl.pallas_call(kernel, out_shape=(jax.ShapeDtypeStruct(tokens.shape, BF),...]
where the time goes in v2:
time: 95.5 us; the launch traced here: 95.2 us
  Pallas kernels  89.9 us (94%)
  local copies, waits for them, and re-layouts  4.72 us (5%)
    pallas_call x1, Pallas kernels, shards(): pl.pallas_call(kernel, out_shape=(jax.ShapeDtypeStruct(tokens.shape[::-1]...  89.9 us
    unnamed x5, local copies, waits for them, and re-layouts  4.72 us

profile of v2, /device:TPU:1, one launch (start us, length us, event | category | flops | bytes accessed | tf_op | source)
XLA Modules:
  0.0 95.2 jit_solution(17831762718876708606)
XLA Ops:
  0.6 89.9 %shard_map.76 = (bf16[448,128]{1,0:T(8,128)(2,1)}, f32[448,512]{1,0:T(8,128)}, f32[448,512]{1,0:T(8,128)}) custom-call(s32[1,128]{1,0:T(1,128)} %bitcast.5, bf16[448,128]{1,0:T(8,128)(2,1)} %bitcast.3, bf16[128,2048]{1,0:T(8,128)(2,1)} %hid_any.1, bf16[448,512]{1,0:T(8,128)(2,1)} %gw_any.1, bf16[448,512]{1,0:T(8,128)(2,1)} %uw_any.1), custom_call_target="tpu_custom_call" | custom-call | tf_op jit(solution)/shard_map/pallas_call | solution.py:357
  90.5 1.6 %copy.11 = bf16[128,448]{0,1:T(8,128)(2,1)} copy(bf16[128,448]{0,1:T(8,128)(2,1)} %bitcast.4) | data formatting | bytes 229376
  92.1 0.0 copy-start
  92.1 2.2 %copy.12 = f32[448,512]{1,0:T(8,128)} copy(f32[448,512]{1,0:T(8,128)} %get-tuple-element.13) | data formatting | bytes 1835008
  94.3 0.0 copy-done
  94.3 0.9 copy.13
Async XLA Ops:
  92.1 2.2 %copy-start = (f32[448,512]{1,0:T(8,128)S(1)}, f32[448,512]{1,0:T(8,128)}, u32[]{:S(2)}) copy-start(f32[448,512]{1,0:T(8,128)} %get-tuple-element.14) | copy-start | bytes 2752516

commit v3 on v2

--- a/solution.py
+++ b/solution.py
@@ -348,6 +348,37 @@
             rs_copy(p, d).wait_send()
             ag_copy(p, d).wait_send()
             relay_copy(p, d).wait_send()
+
+
+def hand_over(arrays):
+    cuts = [(i, part) for i, array in enumerate(arrays) for part in range(array.shape[0] // 112)]
+
+    def body(*refs):
+        count = len(arrays)
+        ins, outs, held = refs[:count], refs[count : 2 * count], refs[2 * count : 3 * count]
+        in_sems, out_sems = refs[3 * count :]
+        loads, stores = [], []
+        for n, (i, part) in enumerate(cuts):
+            rows = pl.ds(part * 112, 112)
+            loads.append(pltpu.make_async_copy(ins[i].at[rows], held[i].at[rows], in_sems.at[n]))
+            stores.append(pltpu.make_async_copy(held[i].at[rows], outs[i].at[rows], out_sems.at[n]))
+        for load in loads:
+            load.start()
+        for load, store in zip(loads, stores):
+            load.wait()
+            store.start()
+        for store in stores:
+            store.wait()
+
+    anywhere = pl.BlockSpec(memory_space=pl.ANY)
+    return pl.pallas_call(
+        body,
+        out_shape=tuple(jax.ShapeDtypeStruct(array.shape, array.dtype) for array in arrays),
+        in_specs=[anywhere] * len(arrays),
+        out_specs=(anywhere,) * len(arrays),
+        scratch_shapes=[pltpu.VMEM(array.shape, array.dtype) for array in arrays]
+        + [pltpu.SemaphoreType.DMA((len(cuts),))] * 2,
+    )(*arrays)
 
 
 def shards(tokens, route_expert, hidden_grad, gate_weight, up_weight):
@@ -403,6 +434,7 @@
             collective_id=0, has_side_effects=True, vmem_limit_bytes=56 * 1024 * 1024
         ),
     )(route_expert.reshape(1, -1), tokens.T, hidden_grad, gate_weight, up_weight)
+    token_grad, gate_grad, up_grad = hand_over((token_grad, gate_grad, up_grad))
     return token_grad.T, gate_grad, up_grad
 
 

time: 95.5 us -> 92.8 us (0.972)
  local copies, waits for them, and re-layouts: 4.72 us -> 0 us
  Pallas kernels: 89.9 us -> 92 us
    unnamed x5 -> x0, local copies, waits for them, and re-layouts: 4.72 us -> none
    pallas_call x0 -> x1, Pallas kernels: none -> 2.51 us  [hand_over(): pl.pallas_call(body, out_shape=tuple((jax.ShapeDtypeStruct(array.shape, a...]
where the time goes in v3:
time: 92.8 us; the launch traced here: 92.6 us
  Pallas kernels  92 us (99%)
    pallas_call x1, Pallas kernels, shards(): pl.pallas_call(kernel, out_shape=(jax.ShapeDtypeStruct(tokens.shape[::-1]...  89.4 us
    pallas_call x1, Pallas kernels, hand_over(): pl.pallas_call(body, out_shape=tuple((jax.ShapeDtypeStruct(array.shape, a...  2.51 us

profile of v3, /device:TPU:1, one launch (start us, length us, event | category | flops | bytes accessed | tf_op | source)
XLA Modules:
  0.0 92.6 jit_solution(17494253828047318499)
XLA Ops:
  0.6 89.4 %shard_map.76 = (bf16[448,128]{1,0:T(8,128)(2,1)}, f32[448,512]{1,0:T(8,128)}, f32[448,512]{1,0:T(8,128)}) custom-call(s32[1,128]{1,0:T(1,128)} %bitcast.4, bf16[448,128]{1,0:T(8,128)(2,1)} %bitcast.3, bf16[128,2048]{1,0:T(8,128)(2,1)} %hid_any.1, bf16[448,512]{1,0:T(8,128)(2,1)} %gw_any.1, bf16[448,512]{1,0:T(8,128)(2,1)} %uw_any.1), custom_call_target="tpu_custom_call" | custom-call | tf_op jit(solution)/shard_map/pallas_call | solution.py:388
  90.1 2.5 %shard_map.77 = (bf16[448,128]{1,0:T(8,128)(2,1)}, f32[448,512]{1,0:T(8,128)}, f32[448,512]{1,0:T(8,128)}) custom-call(bf16[448,128]{1,0:T(8,128)(2,1)} %get-tuple-element.9.refs_0_, f32[448,512]{1,0:T(8,128)} %get-tuple-element.10.refs_1_, f32[448,512]{1,0:T(8,128)} %get-tuple-element.11.refs_2_), custom_call_target="tpu_custom_call" | custom-call | tf_op jit(solution)/shard_map/pallas_call | solution.py:374

commit v4 on v3

--- a/solution.py
+++ b/solution.py
@@ -208,12 +208,11 @@
             if k:
                 y_copy(NY - k).wait_recv()
         mine, other = slots(p)
-        pair = jnp.concatenate([yrecv[other], yrecv[mine]], axis=0)
-        pre = dot(pair, w_ref[...])
-        sib_out[p] = pre[:BLOCK]
+        sib_out[p] = dot(yrecv[other], w_ref[...])
         sib_copy(p).start()
+        pre = dot(yrecv[mine], w_ref[...])
         for i in range(NX):
-            rsum[p, i] = pre[BLOCK:, i * LANE : (i + 1) * LANE]
+            rsum[p, i] = pre[:, i * LANE : (i + 1) * LANE]
 
     def reduce_near(p):
         sib_copy(p).wait_recv()

time: 92.8 us -> 94.3 us (1.016)
  Pallas kernels: 92 us -> 93.4 us
    pallas_call x1, Pallas kernels: 89.4 us -> 90.9 us  [shards(): pl.pallas_call(kernel, out_shape=(jax.ShapeDtypeStruct(tokens.shape[::-1]...]
where the time goes in v4:
time: 94.3 us; the launch traced here: 94.1 us
  Pallas kernels  93.4 us (99%)
    pallas_call x1, Pallas kernels, shards(): pl.pallas_call(kernel, out_shape=(jax.ShapeDtypeStruct(tokens.shape[::-1]...  90.9 us
    pallas_call x1, Pallas kernels, hand_over(): pl.pallas_call(body, out_shape=tuple((jax.ShapeDtypeStruct(array.shape, a...  2.51 us

profile of v4, /device:TPU:1, one launch (start us, length us, event | category | flops | bytes accessed | tf_op | source)
XLA Modules:
  0.0 94.1 jit_solution(13753896208848791349)
XLA Ops:
  0.6 90.9 %shard_map.76 = (bf16[448,128]{1,0:T(8,128)(2,1)}, f32[448,512]{1,0:T(8,128)}, f32[448,512]{1,0:T(8,128)}) custom-call(s32[1,128]{1,0:T(1,128)} %bitcast.4, bf16[448,128]{1,0:T(8,128)(2,1)} %bitcast.3, bf16[128,2048]{1,0:T(8,128)(2,1)} %hid_any.1, bf16[448,512]{1,0:T(8,128)(2,1)} %gw_any.1, bf16[448,512]{1,0:T(8,128)(2,1)} %uw_any.1), custom_call_target="tpu_custom_call" | custom-call | tf_op jit(solution)/shard_map/pallas_call | solution.py:387
  91.6 2.5 %shard_map.77 = (bf16[448,128]{1,0:T(8,128)(2,1)}, f32[448,512]{1,0:T(8,128)}, f32[448,512]{1,0:T(8,128)}) custom-call(bf16[448,128]{1,0:T(8,128)(2,1)} %get-tuple-element.9.refs_0_, f32[448,512]{1,0:T(8,128)} %get-tuple-element.10.refs_1_, f32[448,512]{1,0:T(8,128)} %get-tuple-element.11.refs_2_), custom_call_target="tpu_custom_call" | custom-call | tf_op jit(solution)/shard_map/pallas_call | solution.py:373
